TPU v7x, 256 devices: a whole 4x4x8 slice. The times are simulated.
256 devices in a mesh: wide: 32 (over y, z), narrow: 8 (over x, core).
Axes of the slice: x: 4, y: 4, z: 8, core: 2. Of those that a mesh axis runs over, the one named last changes fastest.
Arguments:
- multipliers: float32 [256, 4, 128, 128], P(('wide', 'narrow')), may hold values from -6 to 6
- residual_in: float32 [256, 4, 128, 128], P(('wide', 'narrow')), may hold values from -6 to 6
- flexibility: float32 [256, 1024, 1024], P(('wide', 'narrow')), may hold values from -2 to 2, as said below
- stiffness: float32 [256, 1024, 1024], P(('wide', 'narrow')), may hold values from -2 to 2, as said below
- body_modes: float32 [256, 6, 1024], P(('wide', 'narrow')), may hold values from -0.8 to 0.8
- mode_counts: int32 [256], P(('wide', 'narrow')), may hold values from 0 to 6
- iface_index: int32 [256, 1024], P(('wide', 'narrow')), may hold values from 0 to 1023, each once within a row
- coarse_inv: float32 [1536, 1536], P('narrow'), may hold values from -2 to 2, as said below
Outputs:
- multipliers_out: float32 [256, 4, 128, 128], P(('wide', 'narrow'))
- residual_out: float32 [256, 4, 128, 128], P(('wide', 'narrow'))
Inputs may be any that keep to these rules, and one draw needn't show every extreme that they name: `iface_index`: each row is a permutation of the local interface unknowns. `flexibility`: symmetric positive definite, diagonal 1 to 2, off-diagonal at most about 0.1. `stiffness`: symmetric positive definite, diagonal 1 to 2, off-diagonal at most about 0.1. `coarse_inv`: symmetric positive definite, diagonal 1 to 2, off-diagonal at most about 0.1.
All inputs are finite; a program needn't handle non-finite values.
Results may differ from a plain program's by a relative error of at most 0.0003.
Values sent between devices are 32-bit elements; how exact they have to be, the bound alone decides.
No kernel may reach another device: no remote copies, remote signals or barrier semaphores. Data moves between devices by JAX's collectives and lax.ppermute only.
A program may use at most 64 MiB of HBM per device.

v0:
```python
import jax
import jax.numpy as jnp
from jax import lax
from jax.sharding import PartitionSpec as P

ITERS = 2


def passed_along(block, axis, distance):
    devices = range(lax.axis_size(axis))
    route = [(i - distance, i) for i in devices if i - distance in devices]
    return lax.ppermute(block, axis, route)


def narrow_move(blocks, toward):
    return passed_along(blocks, "narrow", toward)


def neighbours(blocks, toward):
    along_wide = passed_along(jnp.stack([blocks[0], blocks[2], blocks[3]]), "wide", toward)
    upper = narrow_move(jnp.stack([blocks[1], along_wide[1]]), toward)
    lower = narrow_move(along_wide[2][None], -toward)
    return jnp.stack([along_wide[0], upper[0], upper[1], lower[0]])


def per_device(
    multipliers,
    residual_in,
    flexibility,
    stiffness,
    body_modes,
    mode_counts,
    iface_index,
    coarse_inv,
):
    high = lax.Precision.HIGHEST
    places = iface_index[0]
    slot_size = multipliers.shape[2]
    load_count = multipliers.shape[3]
    iface_size = places.shape[0]
    mode_total = body_modes.shape[1]
    wide_pos = lax.axis_index("wide")
    narrow_pos = lax.axis_index("narrow")
    wide_count = lax.axis_size("wide")
    narrow_count = lax.axis_size("narrow")
    has_wide = wide_pos < wide_count - 1
    has_up = narrow_pos < narrow_count - 1
    has_down = narrow_pos > 0
    valid = jnp.stack([has_wide, has_up, has_wide & has_up, has_wide & has_down]).astype(
        jnp.float32
    )[:, None, None]
    keep = (jnp.arange(mode_total) < mode_counts[0]).astype(jnp.float32)
    masked_modes = body_modes[0] * keep[:, None]
    own_sub = wide_pos * narrow_count + narrow_pos

    def spread_slots(values):
        slots = jnp.concatenate([values, -neighbours(values, 1)], axis=0).reshape(
            iface_size, load_count
        )
        return jnp.zeros((iface_size, load_count), jnp.float32).at[places].set(slots)

    def collect_jumps(local):
        picked = local[places].reshape(8, slot_size, load_count)
        return (picked[:4] - neighbours(picked[4:], -1)) * valid

    def coarse_terms(local):
        return jnp.dot(masked_modes, local, precision=high)

    def coarse_fix(gathered):
        block = jnp.dot(coarse_inv, gathered, precision=high)
        whole = lax.all_gather(block, "narrow", axis=0, tiled=True)
        solved = lax.dynamic_slice_in_dim(whole, own_sub * mode_total, mode_total, 0)
        back = jnp.dot(masked_modes.T, solved, precision=high)
        return collect_jumps(back)

    def project(values):
        gathered = lax.all_gather(
            coarse_terms(spread_slots(values)), ("wide", "narrow"), axis=0, tiled=True
        )
        return values - coarse_fix(gathered)

    def operate(matrix, values):
        return collect_jumps(jnp.dot(matrix, spread_slots(values), precision=high))

    def total_columns(product):
        return lax.psum(jnp.sum(product, axis=(0, 1)), ("wide", "narrow"))

    lam = multipliers[0] * valid
    resid = residual_in[0] * valid
    search = jnp.zeros_like(lam)
    previous = jnp.ones((load_count,), jnp.float32)
    for iteration in range(ITERS):
        projected = project(resid)
        precond = operate(stiffness[0], projected)
        curvature = total_columns(projected * precond)
        along = project(precond)
        if iteration == 0:
            search = along
        else:
            search = along + curvature / previous * search
        image = operate(flexibility[0], search)
        energy = total_columns(search * image)
        step_size = curvature / energy
        lam = lam + step_size * search
        resid = resid - step_size * image
        previous = curvature
    return (lam[None], resid[None])


def solution(mesh):
    in_specs = (
        P(("wide", "narrow"), None, None, None),
        P(("wide", "narrow"), None, None, None),
        P(("wide", "narrow"), None, None),
        P(("wide", "narrow"), None, None),
        P(("wide", "narrow"), None, None),
        P(("wide", "narrow")),
        P(("wide", "narrow"), None),
        P("narrow", None),
    )
    out_specs = (P(("wide", "narrow"), None, None, None), P(("wide", "narrow"), None, None, None))
    return jax.shard_map(
        per_device, mesh=mesh, in_specs=in_specs, out_specs=out_specs, check_vma=False
    )
```

profile of v0, /device:TPU:1, one launch (start us, length us, event | category | flops | bytes accessed | tf_op | source)
XLA Modules:
  0.0 937.9 jit_solution(6721985612013939746)
XLA Ops:
  1.9 4.4 collective-permute-start
  9.9 4.6 collective-permute-start.1
  24.4 66.3 %all-gather = f32[256,6,128]{2,1,0:T(8,128)S(1)} all-gather(f32[1,6,128]{2,1,0:T(8,128)S(1)} %convolution_bitcast_fusion.7), channel_id=1, replica_groups=mesh['wide'=32,'narrow'=8] {'wide','narrow'}, dimensions={0}, use_global_device_ids=true | all-gather | bytes 789504 | tf_op jit(solution)/shard_map/all_gather | solution.py:77
  91.9 13.5 %all_gather.25 = f32[1536,128]{1,0:T(8,128)S(1)} all-gather(f32[192,128]{1,0:T(8,128)S(1)} %convolution_bitcast_fusion.3), channel_id=1, replica_groups=mesh['wide'=32,'narrow'=8] {'narrow'}, dimensions={0}, use_global_device_ids=true | all-gather | bytes 884736 | tf_op jit(solution)/shard_map/all_gather | solution.py:71
  110.7 6.9 collective-permute-done.3
  144.4 6.7 fusion.8
  155.5 5.9 collective-permute-done.9
  163.9 4.8 collective-permute-start.11
  177.8 5.7 collective-permute-start.13
  194.0 64.5 %all-gather.1 = f32[256,6,128]{2,1,0:T(8,128)S(1)} all-gather(f32[1,6,128]{2,1,0:T(8,128)S(1)} %convolution_bitcast_fusion.6), channel_id=1, replica_groups=mesh['wide'=32,'narrow'=8] {'wide','narrow'}, dimensions={0}, use_global_device_ids=true | all-gather | bytes 789504 | tf_op jit(solution)/shard_map/all_gather | solution.py:77
  261.7 13.4 %all_gather.27 = f32[1536,128]{1,0:T(8,128)S(1)} all-gather(f32[192,128]{1,0:T(8,128)S(1)} %convolution_bitcast_fusion.2), channel_id=1, replica_groups=mesh['wide'=32,'narrow'=8] {'narrow'}, dimensions={0}, use_global_device_ids=true | all-gather | bytes 884736 | tf_op jit(solution)/shard_map/all_gather | solution.py:71
  280.3 6.9 collective-permute-done.15
  297.0 4.4 collective-permute-done.18
  314.9 7.5 fusion.14
  329.9 5.9 collective-permute-done.21
  348.7 79.0 %all-reduce = (f32[128]{0:T(128)S(1)}, f32[128]{0:T(128)S(1)}) all-reduce(f32[128]{0:T(128)S(1)} %copy-done.34, f32[128]{0:T(128)S(1)} %get-tuple-element.6), channel_id=1, replica_groups=mesh['wide'=32,'narrow'=8] {'wide','narrow'}, use_global_device_ids=true, to_apply=%region_3.0 | all-reduce | flops 256 | bytes 2048 | tf_op jit(solution)/shard_map/psum | solution.py:86
  434.9 4.4 collective-permute-start.25
  449.7 62.3 %all-gather.2 = f32[256,6,128]{2,1,0:T(8,128)S(1)} all-gather(f32[1,6,128]{2,1,0:T(8,128)S(1)} %convolution_bitcast_fusion.5), channel_id=1, replica_groups=mesh['wide'=32,'narrow'=8] {'wide','narrow'}, dimensions={0}, use_global_device_ids=true | all-gather | bytes 789504 | tf_op jit(solution)/shard_map/all_gather | solution.py:77
  515.3 13.4 %all_gather.29 = f32[1536,128]{1,0:T(8,128)S(1)} all-gather(f32[192,128]{1,0:T(8,128)S(1)} %convolution_bitcast_fusion.1), channel_id=1, replica_groups=mesh['wide'=32,'narrow'=8] {'narrow'}, dimensions={0}, use_global_device_ids=true | all-gather | bytes 884736 | tf_op jit(solution)/shard_map/all_gather | solution.py:71
  534.7 6.9 collective-permute-done.27
  550.5 4.5 collective-permute-done.30
  567.2 6.7 fusion.11
  578.3 5.9 collective-permute-done.33
  586.7 4.3 collective-permute-start.35
  601.3 5.8 collective-permute-start.37
  619.2 70.3 %all-gather.3 = f32[256,6,128]{2,1,0:T(8,128)} all-gather(f32[1,6,128]{2,1,0:T(8,128)S(1)} %convolution_bitcast_fusion.4), channel_id=1, replica_groups=mesh['wide'=32,'narrow'=8] {'wide','narrow'}, dimensions={0}, use_global_device_ids=true | all-gather | bytes 789504 | tf_op jit(solution)/shard_map/all_gather | solution.py:77
  694.0 13.5 %all_gather.31 = f32[1536,128]{1,0:T(8,128)S(1)} all-gather(f32[192,128]{1,0:T(8,128)S(1)} %convolution_bitcast_fusion), channel_id=1, replica_groups=mesh['wide'=32,'narrow'=8] {'narrow'}, dimensions={0}, use_global_device_ids=true | all-gather | bytes 884736 | tf_op jit(solution)/shard_map/all_gather | solution.py:71
  715.5 6.9 collective-permute-done.39
  728.7 75.0 %psum.30 = f32[128]{0:T(128)S(1)} all-reduce(f32[128]{0:T(128)} %get-tuple-element.4), channel_id=1, replica_groups=mesh['wide'=32,'narrow'=8] {'wide','narrow'}, use_global_device_ids=true, to_apply=%region_11.0 | all-reduce | flops 128 | bytes 1024 | tf_op jit(solution)/shard_map/psum | solution.py:86
  823.7 6.7 fusion.17
  836.9 5.9 collective-permute-done.45
  853.3 79.1 %psum.31 = f32[128]{0:T(128)S(1)} all-reduce(f32[128]{0:T(128)} %get-tuple-element.11), channel_id=1, replica_groups=mesh['wide'=32,'narrow'=8] {'wide','narrow'}, use_global_device_ids=true, to_apply=%region_15.0 | all-reduce | flops 128 | bytes 1024 | tf_op jit(solution)/shard_map/psum | solution.py:86
  (306 shorter events, 262.9 us)
Async XLA Ops:
  1.9 7.9 collective-permute-start
  9.9 10.8 %collective-permute-start.1 = (f32[2,128,128]{2,1,0:T(8,128)S(1)}, f32[2,128,128]{2,1,0:T(8,128)S(1)}, u32[]{:S(2)}, u32[]{:S(2)}) collective-permute-start(f32[2,128,128]{2,1,0:T(8,128)S(1)} %pad_maximum_fusion.30), channel_id=1, source_target_pairs={{0,1},{1,2},{2,3},{3,4},{4,5},{5,6},{6,7},{8,9},{9,10},{10,11},{11... | collective-permute-start | bytes 393224 | tf_op jit(solution)/shard_map/ppermute | solution.py:12
  109.4 8.2 collective-permute-start.3
  117.7 6.9 collective-permute-start.4
  124.7 7.0 collective-permute-start.6
  131.8 9.2 collective-permute-start.7
  154.2 7.2 collective-permute-start.9
  162.0 8.0 collective-permute-start.10
  163.9 6.1 collective-permute-start.11
  171.4 6.3 collective-permute-start.12
  177.8 11.3 %collective-permute-start.13 = (f32[2,128,128]{2,1,0:T(8,128)S(1)}, f32[2,128,128]{2,1,0:T(8,128)S(1)}, u32[]{:S(2)}, u32[]{:S(2)}) collective-permute-start(f32[2,128,128]{2,1,0:T(8,128)S(1)} %pad_maximum_fusion.34), channel_id=1, source_target_pairs={{0,1},{1,2},{2,3},{3,4},{4,5},{5,6},{6,7},{8,9},{9,10},{10,11},{11... | collective-permute-start | bytes 393224 | tf_op jit(solution)/shard_map/ppermute | solution.py:12
  279.0 8.2 collective-permute-start.15
  287.9 6.9 collective-permute-start.16
  301.5 8.9 collective-permute-start.19
  328.6 7.2 collective-permute-start.21
  336.5 5.9 collective-permute-start.23
  340.4 6.3 collective-permute-start.22
  434.9 10.0 %collective-permute-start.25 = (f32[2,128,128]{2,1,0:T(8,128)S(1)}, f32[2,128,128]{2,1,0:T(8,128)S(1)}, u32[]{:S(2)}, u32[]{:S(2)}) collective-permute-start(f32[2,128,128]{2,1,0:T(8,128)S(1)} %pad_maximum_fusion.38), channel_id=1, source_target_pairs={{0,1},{1,2},{2,3},{3,4},{4,5},{5,6},{6,7},{8,9},{9,10},{10,11},{11... | collective-permute-start | bytes 393224 | tf_op jit(solution)/shard_map/ppermute | solution.py:12
  533.4 8.2 collective-permute-start.27
  541.6 6.9 collective-permute-start.28
  548.7 6.2 collective-permute-start.30
  555.0 8.9 collective-permute-start.31
  577.0 7.2 collective-permute-start.33
  584.8 7.6 collective-permute-start.34
  594.8 6.5 collective-permute-start.36
  601.3 11.4 %collective-permute-start.37 = (f32[2,128,128]{2,1,0:T(8,128)S(1)}, f32[2,128,128]{2,1,0:T(8,128)S(1)}, u32[]{:S(2)}, u32[]{:S(2)}) collective-permute-start(f32[2,128,128]{2,1,0:T(8,128)S(1)} %pad_maximum_fusion.42), channel_id=1, source_target_pairs={{0,1},{1,2},{2,3},{3,4},{4,5},{5,6},{6,7},{8,9},{9,10},{10,11},{11... | collective-permute-start | bytes 393224 | tf_op jit(solution)/shard_map/ppermute | solution.py:12
  714.2 8.2 collective-permute-start.39
  723.1 82.2 %collective-permute-start.40 = (f32[2,128,128]{2,1,0:T(8,128)S(1)}, f32[2,128,128]{2,1,0:T(8,128)S(1)}, u32[]{:S(2)}, u32[]{:S(2)}) collective-permute-start(f32[2,128,128]{2,1,0:T(8,128)S(1)} %pad_maximum_fusion.43), channel_id=1, source_target_pairs={{1,0},{2,1},{3,2},{4,3},{5,4},{6,5},{7,6},{9,8},{10,9},{11,10},{12... | collective-permute-start | bytes 393224 | tf_op jit(solution)/shard_map/ppermute | solution.py:12
  726.0 79.3 %collective-permute-start.41 = (f32[1,128,128]{2,1,0:T(8,128)S(1)}, f32[1,128,128]{2,1,0:T(8,128)S(1)}, u32[]{:S(2)}, u32[]{:S(2)}) collective-permute-start(f32[1,128,128]{2,1,0:T(8,128)S(1)} %get-tuple-element.80), channel_id=1, source_target_pairs={{0,1},{1,2},{2,3},{3,4},{4,5},{5,6},{6,7},{8,9},{9,10},{10,11},{11... | collective-permute-start | bytes 196616 | tf_op jit(solution)/shard_map/ppermute | solution.py:12
  811.1 8.9 collective-permute-start.43
  835.6 7.2 collective-permute-start.45
  843.5 7.2 collective-permute-start.46
  (54 other events, 2528.1 us)
where the time goes:
time: 948 us; the launch traced here: 938 us
  blocking collectives  550 us (58%)
  starting transfers between devices  129 us (14%)
  waiting for transfers between devices  119 us (13%)
  local copies, waits for them, and re-layouts  71.1 us (7%)
  matrix products  43.5 us (5%)
  other arithmetic  22.2 us (2%)
    all_gather x4, blocking collectives, project(): lax.all_gather(coarse_terms(spread_slots(values)), ('wide', 'narrow'), ax...  263 us
    psum x3, blocking collectives, total_columns(): return lax.psum(jnp.sum(product, axis=(0, 1)), ('wide', 'narrow'))  233 us
    ppermute x48, starting transfers between devices, passed_along(): return lax.ppermute(block, axis, route)  129 us
    ppermute x48, waiting for transfers between devices, passed_along(): return lax.ppermute(block, axis, route)  119 us
    all_gather x4, blocking collectives, coarse_fix(): whole = lax.all_gather(block, 'narrow', axis=0, tiled=True)  53.8 us
    scatter x8, local copies, waits for them, and re-layouts, spread_slots(): jnp.zeros((iface_size, load_count), jnp.float32).at[places].set(slots)  28.6 us
    dot_general x4, matrix products, operate(): return collect_jumps(jnp.dot(matrix, spread_slots(values), precision=high))  27.5 us
    gather x8, local copies, waits for them, and re-layouts, collect_jumps(): picked = local[places].reshape(8, slot_size, load_count)  26 us
  transfers between devices with their start and end apart: 48, of which 31 were waited for; matrix products, arithmetic and copies ran while one was open for 0% of the time, Pallas kernels for 0%

commit v1 on v0

v1 whole, which is shorter than its diff:
```python
import jax
import jax.numpy as jnp
import numpy as np
from jax import lax
from jax.experimental import pallas as pl
from jax.experimental.pallas import tpu as pltpu
from jax.sharding import PartitionSpec as P

GRID_A, GRID_B = 32, 8
SLOT, IFACE, MODES, LOADS = 128, 1024, 6, 128
F32, BF16 = jnp.float32, jnp.bfloat16
HIGH = lax.Precision.HIGHEST

STEP = ((1, 0), (0, 1), (1, 1), (1, -1), (-1, 0), (0, -1), (-1, -1), (-1, 1))
ORDER = (1, 2, 7, 5, 3, 6, 0, 4)
AT = {q: p for p, q in enumerate(ORDER)}
PART = 56


def shift(block, axis, distance):
    size = lax.axis_size(axis)
    return lax.ppermute(block, axis, [(i, (i + distance) % size) for i in range(size)])


def exchange(block, axis):
    return lax.all_to_all(block, axis, 0, 0, tiled=True)


def call(body, outs, *args, scratch=(), smem=(), cost=None):
    specs = [
        pl.BlockSpec(memory_space=pltpu.SMEM if i in smem else pltpu.VMEM) for i in range(len(args))
    ]
    return pl.pallas_call(
        body,
        out_shape=[jax.ShapeDtypeStruct(s, d) for s, d in outs],
        in_specs=specs,
        out_specs=[pl.BlockSpec(memory_space=pltpu.VMEM)] * len(outs),
        scratch_shapes=list(scratch),
        compiler_params=pltpu.CompilerParams(vmem_limit_bytes=40 * 1024 * 1024),
        cost_estimate=None
        if cost is None
        else pl.CostEstimate(flops=cost, bytes_accessed=1 << 20, transcendentals=0),
    )(*args)


def halves(x):
    top = x.astype(BF16)
    return top, (x - top.astype(F32)).astype(BF16)


def thirds(x):
    top, rest = x.astype(BF16), None
    rest = x - top.astype(F32)
    mid = rest.astype(BF16)
    return top, mid, (rest - mid.astype(F32)).astype(BF16)


def mm(a, b):
    return jnp.dot(a, b, preferred_element_type=F32)


def mm_nt(a, b):
    return lax.dot_general(a, b, (((1,), (1,)), ((), ())), preferred_element_type=F32)


def fold(x):
    return x[:, :LOADS] + x[:, LOADS:]


def valid_of(place, q):
    a, b = place[0] + STEP[q][0], place[1] + STEP[q][1]
    return ((a >= 0) & (a < GRID_A) & (b >= 0) & (b < GRID_B)).astype(F32)


def rows(p, count=1):
    return slice(p * SLOT, (p + count) * SLOT)


def prepare_kernel(place, index, modes, matrix, pick, put, mode_slots, top, low):
    values = index[...].astype(F32)
    columns = jnp.transpose(jnp.concatenate([values, jnp.zeros((SLOT - 8, SLOT), F32)], axis=0))
    down = lax.broadcasted_iota(jnp.int32, (IFACE, SLOT), 0).astype(F32)
    across = lax.broadcasted_iota(jnp.int32, (SLOT, IFACE), 1).astype(F32)
    for p, q in enumerate(ORDER):
        pick[:, rows(p)] = (down == values[q : q + 1, :]).astype(F32).astype(BF16)
        put[rows(p), :] = (across == columns[:, q : q + 1]).astype(F32).astype(BF16)
    a, b, c = thirds(modes[...])
    stack = jnp.concatenate([a, b, c, jnp.zeros((8, IFACE), BF16)], axis=0)
    for p, q in enumerate(ORDER):
        part = mm(stack, pick[:, rows(p)])
        mode_slots[:, rows(p)] = (part[0:8] + part[8:16] + part[16:24]) * valid_of(place, q)
    split_into(matrix, top, low)


def split_into(matrix, top, low):
    for p in range(8):
        t, l = halves(matrix[0, rows(p), :])
        top[rows(p), :] = t
        low[rows(p), :] = l


def split_kernel(matrix, top, low):
    split_into(matrix, top, low)


def window_kernel(place, inverse, reorder, out):
    first = jnp.clip(place[0] - 1, 0, GRID_A - 3) * (GRID_B * MODES)
    width = GRID_A * GRID_B * MODES
    down = lax.broadcasted_iota(jnp.int32, (width, 256), 0)
    across = lax.broadcasted_iota(jnp.int32, (width, 256), 1)
    choose = (down == across + first).astype(F32).astype(BF16)
    parts = mm(jnp.concatenate(thirds(inverse[...]), axis=0), choose).astype(BF16)
    wide = jnp.concatenate([parts[0:192], parts[192:384], parts[384:576]], axis=1)
    wide = mm(reorder[...], wide)
    out[...] = wide[:, :256] + wide[:, 256:512] + wide[:, 512:]


def coarse_kernel(target, piece, out):
    across = lax.broadcasted_iota(jnp.int32, (8 * PART, 256), 1)
    goal = target[...]
    choose = (across == goal).astype(F32).astype(BF16)
    parts = mm_nt(choose, jnp.concatenate(thirds(piece[...]), axis=0))
    dots = ((goal == -2) & (across % 8 == 6)).astype(F32)
    out[...] = parts[:, :256] + parts[:, 256:512] + parts[:, 512:] + dots


def first_pass_kernel(resid, from_lower, from_upper, mode_slots, ahead, back):
    ahead[0:128] = resid[0, 0]
    ahead[128:256] = from_lower[128:256]
    ahead[256:384] = from_upper[0:128]
    for i, q in enumerate((0, 2, 3)):
        ahead[384 + 8 * i : 392 + 8 * i] = mode_slots[:, rows(AT[q])]
    for i, q in enumerate((4, 6, 7)):
        back[8 * i : 8 * i + 8] = mode_slots[:, rows(AT[q])]


def first_terms_kernel(place, resid, from_lower, from_west, mode_slots, spread, terms):
    own = {q: resid[0, q] for q in range(4)}
    own[5] = -from_lower[0:128]
    own[4] = -from_west[0:128]
    own[6] = -from_west[128:256]
    own[7] = -from_west[256:384]
    total = jnp.zeros((16, 2 * LOADS), F32)
    for p, q in enumerate(ORDER):
        value = own[q] * valid_of(place, q)
        spread[rows(p), :] = value
        modes = jnp.concatenate(halves(mode_slots[:, rows(p)]), axis=0)
        total += mm(modes, jnp.concatenate(halves(value), axis=1))
    total = fold(total)
    total = total[:8] + total[8:]
    for w in range(GRID_A):
        terms[8 * w : 8 * w + 8] = total


def second_pass_kernel(mode_slots, from_west, from_east, up, down):
    up[0:8] = mode_slots[:, rows(AT[1])]
    up[8:16] = from_east[16:24]
    up[16:24] = from_west[392:400]
    down[0:8] = mode_slots[:, rows(AT[5])]
    down[8:16] = from_east[8:16]
    down[16:24] = from_west[400:408]


def modes_kernel(
    place, mode_slots, from_west, from_east, from_lower, from_upper, squeeze, back_top, back_low, gather
):
    has_east = (place[0] < GRID_A - 1).astype(F32)
    has_west = (place[0] > 0).astype(F32)
    west = {q: from_west[384 + 8 * i : 392 + 8 * i] for i, q in enumerate((0, 2, 3))}
    east = {q: from_east[8 * i : 8 * i + 8] for i, q in enumerate((4, 6, 7))}
    facing = {
        0: east[4],
        4: west[0],
        1: from_upper[0:8],
        2: from_upper[8:16],
        7: from_upper[16:24],
        5: from_lower[0:8],
        3: from_lower[8:16],
        6: from_lower[16:24],
    }
    nothing = jnp.zeros((8, SLOT), F32)
    columns = []
    for p, q in enumerate(ORDER):
        blocks = [nothing] * 16
        blocks[4] = mode_slots[:, rows(p)]
        blocks[(STEP[q][0] + 1) * 3 + STEP[q][1] + 1] = -facing[q] * valid_of(place, q)
        columns.append(jnp.transpose(jnp.concatenate(blocks, axis=0)))
    tall = jnp.concatenate(columns, axis=0)
    parts = [mm(t, squeeze[...]) for t in thirds(tall)]
    t, l = halves(parts[0] + parts[1] + parts[2])
    back_top[...] = t[:, :64]
    back_low[...] = l[:, :64]

    here, plus, minus = [nothing] * 14, [nothing] * 14, [nothing] * 14
    for p in range(8):
        here[p] = mode_slots[:, rows(p)]
    here[8] = -mode_slots[:, rows(AT[5])]
    here[11] = -mode_slots[:, rows(AT[1])]
    plus[6], plus[9], plus[12] = (-east[q] * has_east for q in (4, 6, 7))
    minus[7], minus[13], minus[10] = (-west[q] * has_west for q in (0, 2, 3))
    for j in range(14):
        gather[:, rows(j)] = jnp.concatenate(
            halves(jnp.concatenate([here[j], plus[j], minus[j]], axis=0)), axis=0
        )


def pass_on(own_line, from_lower, from_upper, ahead, back):
    ahead[0:128] = own_line[0:128]
    ahead[128:256] = from_lower[128:256]
    ahead[256:384] = from_upper[128:256]
    back[0:128] = own_line[128:256]
    back[128:256] = from_upper[256:384]
    back[256:384] = from_lower[256:384]


def terms_kernel(up, down, own_line, from_lower, from_upper, gather, dots, ahead, back, terms):
    pass_on(own_line, from_lower, from_upper, ahead, back)
    total = jnp.zeros((48, 2 * LOADS), F32)
    at = 0
    for piece in (up, down, own_line, from_lower, from_upper):
        size = piece.shape[0]
        total += mm(gather[:, at : at + size], jnp.concatenate(halves(piece[...]), axis=1))
        at += size
    total = fold(total)
    total = total[:24] + total[24:]
    total = jnp.concatenate([total[:8] + dots[...], total[8:]], axis=0)
    for w in range(GRID_A):
        terms[24 * w : 24 * w + 24] = total


def pass_kernel(own_line, from_lower, from_upper, ahead, back):
    pass_on(own_line, from_lower, from_upper, ahead, back)


def solve_first_kernel(terms, inverse, out):
    out[...] = jnp.dot(inverse[...], terms[...], precision=HIGH, preferred_element_type=F32)


def solve_kernel(terms, inverse, out):
    parts = []
    for w in range(GRID_A):
        e = terms[24 * w : 24 * w + 8]
        if w > 0:
            e = e + terms[24 * w - 16 : 24 * w - 8]
        if w < GRID_A - 1:
            e = e + terms[24 * w + 40 : 24 * w + 48]
        parts.append(e)
    terms = jnp.concatenate(parts, axis=0)
    out[...] = jnp.dot(inverse[...], terms, precision=HIGH, preferred_element_type=F32)


def jump(place, pieces, p):
    up, down, own_line, from_lower, from_upper, from_west, from_east = pieces
    q = ORDER[p]
    own = (up, down, own_line)[p // 3][rows(p % 3), :]
    source, i = {
        1: (from_upper, 0),
        2: (from_east, 1),
        7: (from_west, 2),
        5: (from_lower, 0),
        3: (from_east, 2),
        6: (from_west, 1),
        0: (from_east, 0),
        4: (from_west, 0),
    }[q]
    return (own - source[rows(i), :]) * valid_of(place, q)


def apply_kernel(kind, *refs):
    n_pieces = 1 if kind == "first" else 7
    place, shares, back_top, back_low, pick, put, top, low = refs[:8]
    pieces = refs[8 : 8 + n_pieces]
    rest = refs[8 + n_pieces :]
    old = None
    if kind in ("residual", "search"):
        old, past = rest[:2]
        rest = rest[2:]
    up, down, own_line, field, total, dots = rest[:6]
    rest = rest[6:]
    jumps = None
    if kind == "residual":
        jumps = rest[0]
        rest = rest[1:]
    left, right = rest

    y = shares[0:PART]
    for n in range(1, GRID_B):
        y = y + shares[PART * n : PART * n + PART]
    inner = y[54:55]
    total[...] = jnp.broadcast_to(inner, (8, LOADS))
    yt, yl = halves(jnp.concatenate([y, jnp.zeros((64 - PART, LOADS), F32)], axis=0))
    both = jnp.concatenate([yt, yl], axis=1)
    if kind == "residual":
        factor = past[0:1] / inner
    if kind == "search":
        factor = inner / past[0:1]

    for c in range(4):
        block = slice(256 * c, 256 * c + 256)
        if kind == "first":
            z = pieces[0][block, :]
        else:
            z = jnp.concatenate([jump(place, pieces, 2 * c), jump(place, pieces, 2 * c + 1)], axis=0)
        if kind == "residual":
            jumps[block, :] = z
        f = z - (fold(mm(back_top[block, :], both)) + mm(back_low[block, :], yt))
        if kind == "residual":
            f = old[block, :] - factor * f
        if kind == "search":
            f = f + factor * old[block, :]
        field[block, :] = f
        left[block, :] = jnp.concatenate(halves(f), axis=1)
    for c in range(4):
        block = slice(256 * c, 256 * c + 256)
        right[block, :] = mm(pick[block, :], left[...]).astype(BF16)
    for c in range(4):
        block = slice(256 * c, 256 * c + 256)
        u = fold(mm(top[block, :], right[...])) + mm(low[block, :], right[:, :LOADS])
        left[block, :] = jnp.concatenate(halves(u), axis=1)
    inner = jnp.zeros((1, LOADS), F32)
    for c in range(4):
        block = slice(256 * c, 256 * c + 256)
        u = fold(mm(put[block, :], left[...]))
        inner = inner + jnp.sum(u * field[block, :], axis=0, keepdims=True)
        for h in range(2):
            p = 2 * c + h
            (up, down, own_line)[p // 3][rows(p % 3), :] = u[rows(h)]
    row = lax.broadcasted_iota(jnp.int32, (8, LOADS), 0)
    dots[...] = jnp.where(row == 6, inner, 0.0)


def last_dots_kernel(gathered, out):
    total = gathered[0:8]
    for w in range(1, GRID_A):
        total = total + gathered[8 * w : 8 * w + 8]
    for n in range(GRID_B):
        out[8 * n : 8 * n + 8] = total


def finish_kernel(
    place, shares, *refs
):
    pieces = refs[:7]
    lam, resid, search, search_2, jumps, gamma, delta, gamma_2, lam_out, resid_out = refs[7:]
    energy = shares[0:8]
    for n in range(1, GRID_B):
        energy = energy + shares[8 * n : 8 * n + 8]
    one = gamma[0:1] / delta[0:1]
    two = gamma_2[0:1] / energy[6:7]
    for q in range(4):
        p = AT[q]
        v = valid_of(place, q)
        lam_out[0, q] = lam[0, q] * v + one * search[rows(p), :] + two * search_2[rows(p), :]
        resid_out[0, q] = resid[0, q] * v - one * jumps[rows(p), :] - two * jump(place, pieces, p)


def reorder_rows():
    out = np.zeros((256, 192), np.float32)
    for b in range(8):
        for a in range(4):
            for m in range(MODES):
                out[b * 32 + a * 8 + m, (a * 8 + b) * MODES + m] = 1
    return out


def squeeze_rows():
    out = np.zeros((128, 128), np.float32)
    for g in range(9):
        for m in range(MODES):
            out[g * 8 + m, g * MODES + m] = 1
    return out


def target_tables():
    da = np.full((8 * PART, 1), 1000, np.int32)
    rest = np.full((8 * PART, 1), -1, np.int32)
    for n in range(8):
        for g in range(9):
            for m in range(MODES):
                b = n + g % 3 - 1
                if 0 <= b < GRID_B:
                    da[n * PART + g * MODES + m] = g // 3 - 1
                    rest[n * PART + g * MODES + m] = b * MODES + m
        rest[n * PART + 54] = -2
    return da, rest


def per_device(
    multipliers,
    residual_in,
    flexibility,
    stiffness,
    body_modes,
    mode_counts,
    iface_index,
    coarse_inv,
):
    wide_pos = lax.axis_index("wide")
    place = jnp.stack([wide_pos, lax.axis_index("narrow")]).astype(jnp.int32)
    square = ((IFACE, IFACE), BF16)
    field = ((IFACE, LOADS), F32)
    three = ((3 * SLOT, LOADS), F32)
    two = ((2 * SLOT, LOADS), F32)
    few = ((8, LOADS), F32)

    from_lower = shift(residual_in[0, 1:3].reshape(2 * SLOT, LOADS), "narrow", 1)
    from_upper = shift(residual_in[0, 3], "narrow", -1)
    keep = (jnp.arange(MODES) < mode_counts[0]).astype(F32)
    modes = jnp.pad(body_modes[0] * keep[:, None], ((0, 2), (0, 0)))
    pick, put, mode_slots, stiff_top, stiff_low = call(
        prepare_kernel,
        [square, square, ((8, IFACE), F32), square, square],
        place,
        iface_index.reshape(8, SLOT),
        modes,
        stiffness,
        smem=(0,),
    )
    window = call(
        window_kernel,
        [((256, 256), F32)],
        place,
        coarse_inv,
        jnp.asarray(reorder_rows(), BF16),
        smem=(0,),
    )[0]
    ahead, back = call(
        first_pass_kernel,
        [((408, LOADS), F32), ((24, LOADS), F32)],
        residual_in,
        from_lower,
        from_upper,
        mode_slots,
    )
    from_west = shift(ahead, "wide", 1)
    from_east = shift(back, "wide", -1)
    piece = exchange(window, "narrow")
    da, rest = target_tables()
    first = jnp.clip(wide_pos - 1, 0, GRID_A - 3)
    row = wide_pos + da
    target = jnp.where((row >= 0) & (row < GRID_A), (row - first) * (GRID_B * MODES) + rest, jnp.minimum(rest, -1))
    inverse = call(coarse_kernel, [((8 * PART, 256), F32)], target, piece)[0]
    spread, terms = call(
        first_terms_kernel,
        [field, ((GRID_A * 8, LOADS), F32)],
        place,
        residual_in,
        from_lower,
        from_west,
        mode_slots,
        smem=(0,),
    )
    up, down = call(second_pass_kernel, [((24, LOADS), F32)] * 2, mode_slots, from_west, from_east)
    modes_lower = shift(up, "narrow", 1)
    modes_upper = shift(down, "narrow", -1)
    flex_top, flex_low = call(split_kernel, [square, square], flexibility)
    terms = exchange(terms, "wide")
    shares = exchange(
        call(solve_first_kernel, [((8 * PART, LOADS), F32)], terms, inverse)[0], "narrow"
    )
    back_top, back_low, gather = call(
        modes_kernel,
        [((IFACE, 64), BF16), ((IFACE, 64), BF16), ((48, 14 * SLOT), BF16)],
        place,
        mode_slots,
        from_west,
        from_east,
        modes_lower,
        modes_upper,
        jnp.asarray(squeeze_rows(), BF16),
        smem=(0,),
    )

    def apply(kind, shares, matrix, pieces, *old):
        outs = [three, three, two, field, few, few] + ([field] if kind == "residual" else [])

        def body(*refs):
            apply_kernel(kind, *refs)

        return call(
            body,
            outs,
            place,
            shares,
            back_top,
            back_low,
            pick,
            put,
            *matrix,
            *pieces,
            *old,
            smem=(0,),
            scratch=[pltpu.VMEM((IFACE, 2 * LOADS), BF16)] * 2,
        )

    def across(up, down):
        return shift(up, "narrow", 1), shift(down, "narrow", -1)

    def coarse(up, down, own_line, dots):
        from_lower, from_upper = across(up, down)
        ahead, back, terms = call(
            terms_kernel,
            [three, three, ((GRID_A * 24, LOADS), F32)],
            up,
            down,
            own_line,
            from_lower,
            from_upper,
            gather,
            dots,
        )
        from_west = shift(ahead, "wide", 1)
        from_east = shift(back, "wide", -1)
        terms = exchange(terms, "wide")
        shares = exchange(
            call(solve_kernel, [((8 * PART, LOADS), F32)], terms, inverse)[0], "narrow"
        )
        return shares, (up, down, own_line, from_lower, from_upper, from_west, from_east)

    stiff, flex = (stiff_top, stiff_low), (flex_top, flex_low)
    up, down, own_line, proj, _, dots = apply("first", shares, stiff, (spread,))
    shares, pieces = coarse(up, down, own_line, dots)
    up, down, own_line, search, gamma, dots = apply("plain", shares, flex, pieces)
    shares, pieces = coarse(up, down, own_line, dots)
    up, down, own_line, _, delta, dots, image = apply("residual", shares, stiff, pieces, proj, gamma)
    shares, pieces = coarse(up, down, own_line, dots)
    up, down, own_line, search_2, gamma_2, dots = apply("search", shares, flex, pieces, search, gamma)

    from_lower, from_upper = across(up, down)
    ahead, back = call(pass_kernel, [three, three], own_line, from_lower, from_upper)
    from_west = shift(ahead, "wide", 1)
    from_east = shift(back, "wide", -1)
    gathered = exchange(jnp.tile(dots, (GRID_A, 1)), "wide")
    shares = exchange(call(last_dots_kernel, [((64, LOADS), F32)], gathered)[0], "narrow")
    out = ((1, 4, SLOT, LOADS), F32)
    return tuple(
        call(
            finish_kernel,
            [out, out],
            place,
            shares,
            up,
            down,
            own_line,
            from_lower,
            from_upper,
            from_west,
            from_east,
            multipliers,
            residual_in,
            search,
            search_2,
            image,
            gamma,
            delta,
            gamma_2,
            smem=(0,),
        )
    )


def solution(mesh):
    both = ("wide", "narrow")
    in_specs = (
        P(both, None, None, None),
        P(both, None, None, None),
        P(both, None, None),
        P(both, None, None),
        P(both, None, None),
        P(both),
        P(both, None),
        P("narrow", None),
    )
    out_specs = (P(both, None, None, None), P(both, None, None, None))
    return jax.shard_map(
        per_device, mesh=mesh, in_specs=in_specs, out_specs=out_specs, check_vma=False
    )
```

time: 948 us -> 310 us (0.33)
  blocking collectives: 550 us -> 64.9 us
  waiting for transfers between devices: 119 us -> 54.3 us
  starting transfers between devices: 129 us -> 78.6 us
  matrix products: 43.5 us -> 0 us
  Pallas kernels: 0 us -> 30.8 us
  other arithmetic: 22.2 us -> 1.38 us
    all_gather x8 -> x0, blocking collectives: 317 us -> none  [the longest x4 263 us: project(): lax.all_gather(coarse_terms(spread_slots(values)), ('wide', 'narrow'), ax...]
    psum x3 -> x0, blocking collectives: 233 us -> none  [total_columns(): return lax.psum(jnp.sum(product, axis=(0, 1)), ('wide', 'narrow'))]
    ppermute x48 -> x22, starting transfers between devices: 129 us -> 34.8 us  [shift(): lax.ppermute(block, axis, [(i, (i + distance) % size) for i in range(size)])]
    ppermute x48 -> x22, waiting for transfers between devices: 119 us -> 42.5 us  [shift(): lax.ppermute(block, axis, [(i, (i + distance) % size) for i in range(size)])]
    unnamed x78 -> x188, local copies, waits for them, and re-layouts: 5.57 us -> 73.8 us
    all_to_all x0 -> x4, blocking collectives: none -> 64.9 us  [exchange(): return lax.all_to_all(block, axis, 0, 0, tiled=True)]
    all_to_all x0 -> x7, starting transfers between devices: none -> 43.8 us  [exchange(): return lax.all_to_all(block, axis, 0, 0, tiled=True)]
    dot_general x16 -> x0, matrix products: 43.5 us -> none  [the longest x4 27.5 us: operate(): return collect_jumps(jnp.dot(matrix, spread_slots(values), precision=high))]
  transfers between devices with their start and end apart: 48 -> 29, of which waited for: 31 -> 14; matrix products, arithmetic and copies ran while one was open for 0% -> 1% of each run, Pallas kernels for 0% -> 3%
where the time goes in v1:
time: 310 us; the launch traced here: 308 us
  starting transfers between devices  78.6 us (25%)
  local copies, waits for them, and re-layouts  76.2 us (25%)
  blocking collectives  64.9 us (21%)
  waiting for transfers between devices  54.3 us (18%)
  Pallas kernels  30.8 us (10%)
    unnamed x188, local copies, waits for them, and re-layouts  73.8 us
    all_to_all x4, blocking collectives, exchange(): return lax.all_to_all(block, axis, 0, 0, tiled=True)  64.9 us
    all_to_all x7, starting transfers between devices, exchange(): return lax.all_to_all(block, axis, 0, 0, tiled=True)  43.8 us
    ppermute x22, waiting for transfers between devices, shift(): lax.ppermute(block, axis, [(i, (i + distance) % size) for i in range(size)])  42.5 us
    ppermute x22, starting transfers between devices, shift(): lax.ppermute(block, axis, [(i, (i + distance) % size) for i in range(size)])  34.8 us
    pallas_call x22, Pallas kernels, call(): pl.pallas_call(body, out_shape=[jax.ShapeDtypeStruct(s, d) for s, d in ou...  30.8 us
    all_to_all x7, waiting for transfers between devices, exchange(): return lax.all_to_all(block, axis, 0, 0, tiled=True)  11.7 us
  transfers between devices with their start and end apart: 29, of which 14 were waited for; matrix products, arithmetic and copies ran while one was open for 1% of the time, Pallas kernels for 3%

profile of v1, /device:TPU:1, one launch (start us, length us, event | category | flops | bytes accessed | tf_op | source)
XLA Modules:
  0.0 307.9 jit_solution(5658574429506528672)
XLA Ops:
  1.5 3.2 %collective-permute-start.1 = (f32[128,128]{1,0:T(8,128)S(1)}, f32[128,128]{1,0:T(8,128)S(1)}, u32[]{:S(2)}, u32[]{:S(2)}) collective-permute-start(f32[128,128]{1,0:T(8,128)S(1)} %slice_bitcast_fusion), channel_id=1, source_target_pairs={{0,7},{1,0},{2,1},{3,2},{4,3},{5,4},{6,5},{7,6},{8,15},{9,8},{10,9... | collective-permute-start | bytes 196616 | tf_op jit(solution)/shard_map/ppermute | solution.py:22
  10.2 4.7 %all-to-all-start.1 = ((f32[8,32,256]{2,1,0:T(8,128)}), f32[8,32,256]{2,1,0:T(8,128)S(1)}, u32[]{:S(2)}, u32[]{:S(2)}) async-start(f32[8,32,256]{2,1,0:T(8,128)} %bitcast.8), calls=%async_computation.1 | async-start | bytes 524288 | tf_op jit(solution)/shard_map/all_to_all | solution.py:26
  17.8 3.0 shard_map.131
  26.6 11.9 %collective-permute-done.2.from_west = f32[408,128]{1,0:T(8,128)S(1)} collective-permute-done((f32[408,128]{1,0:T(8,128)S(1)}, f32[408,128]{1,0:T(8,128)S(1)}, u32[]{:S(2)}, u32[]{:S(2)}) %collective-permute-start.2) | collective-permute-done | bytes 208928 | tf_op jit(solution)/shard_map/ppermute | solution.py:22
  40.8 5.9 %all-to-all-start = ((f32[32,8,128]{2,1,0:T(8,128)}), f32[32,8,128]{2,1,0:T(8,128)}, u32[]{:S(2)}, u32[]{:S(2)}) async-start(f32[32,8,128]{2,1,0:T(8,128)} %bitcast.6), calls=%async_computation | async-start | bytes 262144 | tf_op jit(solution)/shard_map/all_to_all | solution.py:26
  48.4 7.5 %all-to-all-done = f32[32,8,128]{2,1,0:T(8,128)} async-done(((f32[32,8,128]{2,1,0:T(8,128)}), f32[32,8,128]{2,1,0:T(8,128)}, u32[]{:S(2)}, u32[]{:S(2)}) %all-to-all-start) | async-done | bytes 131104 | tf_op jit(solution)/shard_map/all_to_all | solution.py:26
  58.0 6.8 %all-to-all-start.2 = ((f32[8,56,128]{2,1,0:T(8,128)}), f32[8,56,128]{2,1,0:T(8,128)}, u32[]{:S(2)}, u32[]{:S(2)}) async-start(f32[8,56,128]{2,1,0:T(8,128)} %bitcast.10), calls=%async_computation.2 | async-start | bytes 458752 | tf_op jit(solution)/shard_map/all_to_all | solution.py:26
  67.5 2.8 collective-permute-start.4
  82.4 4.1 %shard_map.139 = (f32[384,128]{1,0:T(8,128)S(1)}, f32[384,128]{1,0:T(8,128)S(1)}, f32[256,128]{1,0:T(8,128)S(1)}, f32[1024,128]{1,0:T(8,128)S(1)}, f32[8,128]{1,0:T(8,128)}, /*index=5*/f32[8,128]{1,0:T(8,128)S(1)}) custom-call(s32[2]{0:T(128)S(1)} %pad_add_fusion.place.refs_0_, f32[448,128]{1,0:T(8,128)} %bitcast.11.refs_1_, ...), custom_call_target="tpu_custom_call" | custom-call | tf_op jit(solution)/shard_map/pallas_call | solution.py:33
  89.2 2.8 collective-permute-done.7.from_upper.refs_12_
  93.6 17.4 %all_to_all.118 = f32[32,24,128]{2,1,0:T(8,128)S(1)} all-to-all(f32[32,24,128]{2,1,0:T(8,128)S(1)} %bitcast.41), channel_id=1, replica_groups=mesh['wide'=32,'narrow'=8] {'wide'}, dimensions={0} | all-to-all | bytes 786432 | tf_op jit(solution)/shard_map/all_to_all | solution.py:26
  112.3 7.5 %all-to-all-start.4 = ((f32[8,56,128]{2,1,0:T(8,128)}), f32[8,56,128]{2,1,0:T(8,128)}, u32[]{:S(2)}, u32[]{:S(2)}) async-start(f32[8,56,128]{2,1,0:T(8,128)} %bitcast.35), calls=%async_computation.4 | async-start | bytes 458752 | tf_op jit(solution)/shard_map/all_to_all | solution.py:26
  121.9 2.6 collective-permute-start.9
  142.8 3.6 %shard_map.143 = (f32[384,128]{1,0:T(8,128)S(1)}, f32[384,128]{1,0:T(8,128)S(1)}, f32[256,128]{1,0:T(8,128)S(1)}, f32[1024,128]{1,0:T(8,128)S(1)}, f32[8,128]{1,0:T(8,128)S(1)}, /*index=5*/f32[8,128]{1,0:T(8,128)S(1)}) custom-call(s32[2]{0:T(128)S(1)} %pad_add_fusion.place.refs_0_, f32[448,128]{1,0:T(8,128)} %bitcast.15.refs_1_, ...), custom_call_target="tpu_custom_call" | custom-call | tf_op jit(solution)/shard_map/pallas_call | solution.py:33
  149.5 2.6 collective-permute-done.10.from_lower.refs_11_
  152.1 2.5 collective-permute-done.11.from_upper.refs_12_
  156.2 17.7 %all_to_all.119 = f32[32,24,128]{2,1,0:T(8,128)S(1)} all-to-all(f32[32,24,128]{2,1,0:T(8,128)S(1)} %bitcast.42), channel_id=1, replica_groups=mesh['wide'=32,'narrow'=8] {'wide'}, dimensions={0} | all-to-all | bytes 786432 | tf_op jit(solution)/shard_map/all_to_all | solution.py:26
  175.2 6.6 %all-to-all-start.6 = ((f32[8,56,128]{2,1,0:T(8,128)}), f32[8,56,128]{2,1,0:T(8,128)}, u32[]{:S(2)}, u32[]{:S(2)}) async-start(f32[8,56,128]{2,1,0:T(8,128)} %bitcast.37), calls=%async_computation.6 | async-start | bytes 458752 | tf_op jit(solution)/shard_map/all_to_all | solution.py:26
  183.6 2.9 collective-permute-start.13
  186.5 5.2 %collective-permute-done.12.refs_13_ = f32[384,128]{1,0:T(8,128)S(1)} collective-permute-done((f32[384,128]{1,0:T(8,128)}, f32[384,128]{1,0:T(8,128)S(1)}, u32[]{:S(2)}, u32[]{:S(2)}) %collective-permute-start.12) | collective-permute-done | bytes 196640 | tf_op jit(solution)/shard_map/ppermute | solution.py:22
  205.4 3.8 %shard_map.146 = (f32[384,128]{1,0:T(8,128)S(1)}, f32[384,128]{1,0:T(8,128)S(1)}, f32[256,128]{1,0:T(8,128)S(1)}, f32[1024,128]{1,0:T(8,128)}, f32[8,128]{1,0:T(...) custom-call(s32[2]{0:T(128)S(1)} %pad_add_fusion.place.refs_0_, f32[448,128]{1,0:T(8,128)} %bitcast.19.refs_1_, ...), custom_call_target="tpu_custom_call" | custom-call | tf_op jit(solution)/shard_map/pallas_call | solution.py:33
  211.3 2.6 collective-permute-done.14.from_lower.refs_11_
  213.9 2.5 collective-permute-done.15.from_upper.refs_12_
  218.1 18.2 %all_to_all.120 = f32[32,24,128]{2,1,0:T(8,128)S(1)} all-to-all(f32[32,24,128]{2,1,0:T(8,128)S(1)} %bitcast.40), channel_id=1, replica_groups=mesh['wide'=32,'narrow'=8] {'wide'}, dimensions={0} | all-to-all | bytes 786432 | tf_op jit(solution)/shard_map/all_to_all | solution.py:26
  237.5 6.6 %all-to-all-start.8 = ((f32[8,56,128]{2,1,0:T(8,128)}), f32[8,56,128]{2,1,0:T(8,128)S(1)}, u32[]{:S(2)}, u32[]{:S(2)}) async-start(f32[8,56,128]{2,1,0:T(8,128)} %bitcast.36), calls=%async_computation.8 | async-start | bytes 458752 | tf_op jit(solution)/shard_map/all_to_all | solution.py:26
  245.8 3.1 collective-permute-start.17
  248.9 5.3 %collective-permute-done.16.refs_13_ = f32[384,128]{1,0:T(8,128)S(1)} collective-permute-done((f32[384,128]{1,0:T(8,128)}, f32[384,128]{1,0:T(8,128)S(1)}, u32[]{:S(2)}, u32[]{:S(2)}) %collective-permute-start.16) | collective-permute-done | bytes 196640 | tf_op jit(solution)/shard_map/ppermute | solution.py:22
  267.8 3.9 %shard_map.149 = (f32[384,128]{1,0:T(8,128)}, f32[384,128]{1,0:T(8,128)}, f32[256,128]{1,0:T(8,128)S(1)}, f32[1024,128]{1,0:T(8,128)S(1)}, f32[8,128]{1,0:T(8,128)S(1)}, /*index=5*/f32[8,128]{1,0:T(8,128)S(1)}) custom-call(s32[2]{0:T(128)S(1)} %pad_add_fusion.place.refs_0_, f32[448,128]{1,0:T(8,128)S(1)} %bitcast.38, ...), custom_call_target="tpu_custom_call" | custom-call | tf_op jit(solution)/shard_map/pallas_call | solution.py:33
  275.2 5.8 %all-to-all-start.9 = ((f32[32,8,128]{2,1,0:T(8,128)}), f32[32,8,128]{2,1,0:T(8,128)S(1)}, u32[]{:S(2)}, u32[]{:S(2)}) async-start(f32[32,8,128]{2,1,0:T(8,128)} %tile.2), calls=%async_computation.9 | async-start | bytes 262144 | tf_op jit(solution)/shard_map/all_to_all | solution.py:26
  282.4 3.6 %collective-permute-start.21 = (f32[384,128]{1,0:T(8,128)S(1)}, f32[384,128]{1,0:T(8,128)S(1)}, u32[]{:S(2)}, u32[]{:S(2)}) collective-permute-start(f32[384,128]{1,0:T(8,128)S(1)} %get-tuple-element.97), channel_id=1, source_target_pairs={{0,248},{8,0},{16,8},{24,16},{32,24},{40,32},{48,40},{56,48},{64,5... | collective-permute-start | bytes 589832 | tf_op jit(solution)/shard_map/ppermute | solution.py:22
  285.9 4.2 %all-to-all-done.9 = f32[32,8,128]{2,1,0:T(8,128)S(1)} async-done(((f32[32,8,128]{2,1,0:T(8,128)}), f32[32,8,128]{2,1,0:T(8,128)S(1)}, u32[]{:S(2)}, u32[]{:S(2)}) %all-to-all-start.9) | async-done | bytes 131104 | tf_op jit(solution)/shard_map/all_to_all | solution.py:26
  290.2 11.6 %all_to_all.121 = f32[8,8,128]{2,1,0:T(8,128)S(1)} all-to-all(f32[8,8,128]{2,1,0:T(8,128)S(1)} %bitcast.44), channel_id=1, replica_groups=mesh['wide'=32,'narrow'=8] {'narrow'}, dimensions={0} | all-to-all | bytes 65536 | tf_op jit(solution)/shard_map/all_to_all | solution.py:26
  (248 shorter events, 113.7 us)
Async XLA Ops:
  1.5 23.4 %collective-permute-start.1 = (f32[128,128]{1,0:T(8,128)S(1)}, f32[128,128]{1,0:T(8,128)S(1)}, u32[]{:S(2)}, u32[]{:S(2)}) collective-permute-start(f32[128,128]{1,0:T(8,128)S(1)} %slice_bitcast_fusion), channel_id=1, source_target_pairs={{0,7},{1,0},{2,1},{3,2},{4,3},{5,4},{6,5},{7,6},{8,15},{9,8},{10,9... | collective-permute-start | bytes 196616 | tf_op jit(solution)/shard_map/ppermute | solution.py:22
  5.7 19.2 %collective-permute-start = (f32[256,128]{1,0:T(8,128)S(1)}, f32[256,128]{1,0:T(8,128)S(1)}, u32[]{:S(2)}, u32[]{:S(2)}) collective-permute-start(f32[256,128]{1,0:T(8,128)S(1)} %bitcast.46), channel_id=1, source_target_pairs={{0,1},{1,2},{2,3},{3,4},{4,5},{5,6},{6,7},{7,0},{8,9},{9,10},{10,1... | collective-permute-start | bytes 393224 | tf_op jit(solution)/shard_map/ppermute | solution.py:22
  10.2 30.6 %all-to-all-start.1 = ((f32[8,32,256]{2,1,0:T(8,128)}), f32[8,32,256]{2,1,0:T(8,128)S(1)}, u32[]{:S(2)}, u32[]{:S(2)}) async-start(f32[8,32,256]{2,1,0:T(8,128)} %bitcast.8), calls=%async_computation.1 | async-start | bytes 524288 | tf_op jit(solution)/shard_map/all_to_all | solution.py:26
  24.9 13.6 %collective-permute-start.2 = (f32[408,128]{1,0:T(8,128)S(1)}, f32[408,128]{1,0:T(8,128)S(1)}, u32[]{:S(2)}, u32[]{:S(2)}) collective-permute-start(f32[408,128]{1,0:T(8,128)S(1)} %get-tuple-element.53), channel_id=1, source_target_pairs={{0,8},{8,16},{16,24},{24,32},{32,40},{40,48},{48,56},{56,64},{64,7... | collective-permute-start | bytes 626696 | tf_op jit(solution)/shard_map/ppermute | solution.py:22
  40.8 15.1 %all-to-all-start = ((f32[32,8,128]{2,1,0:T(8,128)}), f32[32,8,128]{2,1,0:T(8,128)}, u32[]{:S(2)}, u32[]{:S(2)}) async-start(f32[32,8,128]{2,1,0:T(8,128)} %bitcast.6), calls=%async_computation | async-start | bytes 262144 | tf_op jit(solution)/shard_map/all_to_all | solution.py:26
  58.0 18.6 %all-to-all-start.2 = ((f32[8,56,128]{2,1,0:T(8,128)}), f32[8,56,128]{2,1,0:T(8,128)}, u32[]{:S(2)}, u32[]{:S(2)}) async-start(f32[8,56,128]{2,1,0:T(8,128)} %bitcast.10), calls=%async_computation.2 | async-start | bytes 458752 | tf_op jit(solution)/shard_map/all_to_all | solution.py:26
  64.7 2.8 collective-permute-start.3
  67.5 3.6 %collective-permute-start.4 = (f32[24,128]{1,0:T(8,128)S(1)}, f32[24,128]{1,0:T(8,128)S(1)}, u32[]{:S(2)}, u32[]{:S(2)}) collective-permute-start(f32[24,128]{1,0:T(8,128)S(1)} %get-tuple-element.56), channel_id=1, source_target_pairs={{0,1},{1,2},{2,3},{3,4},{4,5},{5,6},{6,7},{7,0},{8,9},{9,10},{10,1... | collective-permute-start | bytes 36872 | tf_op jit(solution)/shard_map/ppermute | solution.py:22
  70.3 3.1 %collective-permute-start.5 = (f32[24,128]{1,0:T(8,128)S(1)}, f32[24,128]{1,0:T(8,128)S(1)}, u32[]{:S(2)}, u32[]{:S(2)}) collective-permute-start(f32[24,128]{1,0:T(8,128)S(1)} %get-tuple-element.57), channel_id=1, source_target_pairs={{0,7},{1,0},{2,1},{3,2},{4,3},{5,4},{6,5},{7,6},{8,15},{9,8},{10,9... | collective-permute-start | bytes 36872 | tf_op jit(solution)/shard_map/ppermute | solution.py:22
  86.5 2.7 collective-permute-start.6
  86.6 5.4 %collective-permute-start.7 = (f32[384,128]{1,0:T(8,128)S(1)}, f32[384,128]{1,0:T(8,128)S(1)}, u32[]{:S(2)}, u32[]{:S(2)}) collective-permute-start(f32[384,128]{1,0:T(8,128)S(1)} %get-tuple-element.66.down.refs_9_), channel_id=1, source_target_pairs={{0,7},{1,0},{2,1},{3,2},{4,3},{5,4},{6,5},{7,6},{8,15},{9,8},{10,9... | collective-permute-start | bytes 589832 | tf_op jit(solution)/shard_map/ppermute | solution.py:22
  112.3 19.3 %all-to-all-start.4 = ((f32[8,56,128]{2,1,0:T(8,128)}), f32[8,56,128]{2,1,0:T(8,128)}, u32[]{:S(2)}, u32[]{:S(2)}) async-start(f32[8,56,128]{2,1,0:T(8,128)} %bitcast.35), calls=%async_computation.4 | async-start | bytes 458752 | tf_op jit(solution)/shard_map/all_to_all | solution.py:26
  119.8 10.4 %collective-permute-start.8 = (f32[384,128]{1,0:T(8,128)}, f32[384,128]{1,0:T(8,128)S(1)}, u32[]{:S(2)}, u32[]{:S(2)}) collective-permute-start(f32[384,128]{1,0:T(8,128)} %copy-done.88), channel_id=1, source_target_pairs={{0,8},{8,16},{16,24},{24,32},{32,40},{40,48},{48,56},{56,64},{64,7... | collective-permute-start | bytes 589832 | tf_op jit(solution)/shard_map/ppermute | solution.py:22
  121.9 9.0 %collective-permute-start.9 = (f32[384,128]{1,0:T(8,128)}, f32[384,128]{1,0:T(8,128)S(1)}, u32[]{:S(2)}, u32[]{:S(2)}) collective-permute-start(f32[384,128]{1,0:T(8,128)} %copy-done.86), channel_id=1, source_target_pairs={{0,248},{8,0},{16,8},{24,16},{32,24},{40,32},{48,40},{56,48},{64,5... | collective-permute-start | bytes 589832 | tf_op jit(solution)/shard_map/ppermute | solution.py:22
  147.3 4.8 %collective-permute-start.10 = (f32[384,128]{1,0:T(8,128)S(1)}, f32[384,128]{1,0:T(8,128)S(1)}, u32[]{:S(2)}, u32[]{:S(2)}) collective-permute-start(f32[384,128]{1,0:T(8,128)S(1)} %get-tuple-element.75.up.refs_8_), channel_id=1, source_target_pairs={{0,1},{1,2},{2,3},{3,4},{4,5},{5,6},{6,7},{7,0},{8,9},{9,10},{10,1... | collective-permute-start | bytes 589832 | tf_op jit(solution)/shard_map/ppermute | solution.py:22
  149.5 5.1 %collective-permute-start.11 = (f32[384,128]{1,0:T(8,128)S(1)}, f32[384,128]{1,0:T(8,128)S(1)}, u32[]{:S(2)}, u32[]{:S(2)}) collective-permute-start(f32[384,128]{1,0:T(8,128)S(1)} %get-tuple-element.76.down.refs_9_), channel_id=1, source_target_pairs={{0,7},{1,0},{2,1},{3,2},{4,3},{5,4},{6,5},{7,6},{8,15},{9,8},{10,9... | collective-permute-start | bytes 589832 | tf_op jit(solution)/shard_map/ppermute | solution.py:22
  175.2 17.9 %all-to-all-start.6 = ((f32[8,56,128]{2,1,0:T(8,128)}), f32[8,56,128]{2,1,0:T(8,128)}, u32[]{:S(2)}, u32[]{:S(2)}) async-start(f32[8,56,128]{2,1,0:T(8,128)} %bitcast.37), calls=%async_computation.6 | async-start | bytes 458752 | tf_op jit(solution)/shard_map/all_to_all | solution.py:26
  181.7 10.0 %collective-permute-start.12 = (f32[384,128]{1,0:T(8,128)}, f32[384,128]{1,0:T(8,128)S(1)}, u32[]{:S(2)}, u32[]{:S(2)}) collective-permute-start(f32[384,128]{1,0:T(8,128)} %copy-done.91), channel_id=1, source_target_pairs={{0,8},{8,16},{16,24},{24,32},{32,40},{40,48},{48,56},{56,64},{64,7... | collective-permute-start | bytes 589832 | tf_op jit(solution)/shard_map/ppermute | solution.py:22
  183.6 8.8 %collective-permute-start.13 = (f32[384,128]{1,0:T(8,128)}, f32[384,128]{1,0:T(8,128)S(1)}, u32[]{:S(2)}, u32[]{:S(2)}) collective-permute-start(f32[384,128]{1,0:T(8,128)} %copy-done.89), channel_id=1, source_target_pairs={{0,248},{8,0},{16,8},{24,16},{32,24},{40,32},{48,40},{56,48},{64,5... | collective-permute-start | bytes 589832 | tf_op jit(solution)/shard_map/ppermute | solution.py:22
  209.2 27.6 %copy-start.31 = (f32[384,128]{1,0:T(8,128)}, f32[384,128]{1,0:T(8,128)S(1)}, u32[]{:S(2)}) copy-start(f32[384,128]{1,0:T(8,128)S(1)} %get-tuple-element.85.down.refs_9_) | copy-start | bytes 589828
  209.2 27.6 %copy-start.53 = (f32[256,128]{1,0:T(8,128)}, f32[256,128]{1,0:T(8,128)S(1)}, u32[]{:S(2)}) copy-start(f32[256,128]{1,0:T(8,128)S(1)} %get-tuple-element.86.own_line.refs_10_) | copy-start | bytes 393220
  209.2 27.6 %copy-start.63 = (f32[1024,128]{1,0:T(8,128)}, f32[1024,128]{1,0:T(8,128)S(1)}, u32[]{:S(2)}) copy-start(f32[1024,128]{1,0:T(8,128)S(1)} %get-tuple-element.99.refs_11_) | copy-start | bytes 1572868
  209.2 4.7 %collective-permute-start.14 = (f32[384,128]{1,0:T(8,128)S(1)}, f32[384,128]{1,0:T(8,128)S(1)}, u32[]{:S(2)}, u32[]{:S(2)}) collective-permute-start(f32[384,128]{1,0:T(8,128)S(1)} %get-tuple-element.84.up.refs_8_), channel_id=1, source_target_pairs={{0,1},{1,2},{2,3},{3,4},{4,5},{5,6},{6,7},{7,0},{8,9},{9,10},{10,1... | collective-permute-start | bytes 589832 | tf_op jit(solution)/shard_map/ppermute | solution.py:22
  211.3 5.1 %collective-permute-start.15 = (f32[384,128]{1,0:T(8,128)S(1)}, f32[384,128]{1,0:T(8,128)S(1)}, u32[]{:S(2)}, u32[]{:S(2)}) collective-permute-start(f32[384,128]{1,0:T(8,128)S(1)} %get-tuple-element.85.down.refs_9_), channel_id=1, source_target_pairs={{0,7},{1,0},{2,1},{3,2},{4,3},{5,4},{6,5},{7,6},{8,15},{9,8},{10,9... | collective-permute-start | bytes 589832 | tf_op jit(solution)/shard_map/ppermute | solution.py:22
  237.5 18.0 %all-to-all-start.8 = ((f32[8,56,128]{2,1,0:T(8,128)}), f32[8,56,128]{2,1,0:T(8,128)S(1)}, u32[]{:S(2)}, u32[]{:S(2)}) async-start(f32[8,56,128]{2,1,0:T(8,128)} %bitcast.36), calls=%async_computation.8 | async-start | bytes 458752 | tf_op jit(solution)/shard_map/all_to_all | solution.py:26
  244.1 10.1 %collective-permute-start.16 = (f32[384,128]{1,0:T(8,128)}, f32[384,128]{1,0:T(8,128)S(1)}, u32[]{:S(2)}, u32[]{:S(2)}) collective-permute-start(f32[384,128]{1,0:T(8,128)} %copy-done.90), channel_id=1, source_target_pairs={{0,8},{8,16},{16,24},{24,32},{32,40},{40,48},{48,56},{56,64},{64,7... | collective-permute-start | bytes 589832 | tf_op jit(solution)/shard_map/ppermute | solution.py:22
  245.8 9.0 %collective-permute-start.17 = (f32[384,128]{1,0:T(8,128)}, f32[384,128]{1,0:T(8,128)S(1)}, u32[]{:S(2)}, u32[]{:S(2)}) collective-permute-start(f32[384,128]{1,0:T(8,128)} %copy-done.87), channel_id=1, source_target_pairs={{0,248},{8,0},{16,8},{24,16},{32,24},{40,32},{48,40},{56,48},{64,5... | collective-permute-start | bytes 589832 | tf_op jit(solution)/shard_map/ppermute | solution.py:22
  272.5 8.5 %collective-permute-start.18 = (f32[384,128]{1,0:T(8,128)}, f32[384,128]{1,0:T(8,128)S(1)}, u32[]{:S(2)}, u32[]{:S(2)}) collective-permute-start(f32[384,128]{1,0:T(8,128)} %get-tuple-element.93.refs_0_), channel_id=1, source_target_pairs={{0,1},{1,2},{2,3},{3,4},{4,5},{5,6},{6,7},{7,0},{8,9},{9,10},{10,1... | collective-permute-start | bytes 589832 | tf_op jit(solution)/shard_map/ppermute | solution.py:22
  274.6 6.5 %collective-permute-start.19 = (f32[384,128]{1,0:T(8,128)}, f32[384,128]{1,0:T(8,128)S(1)}, u32[]{:S(2)}, u32[]{:S(2)}) collective-permute-start(f32[384,128]{1,0:T(8,128)} %get-tuple-element.94.refs_1_), channel_id=1, source_target_pairs={{0,7},{1,0},{2,1},{3,2},{4,3},{5,4},{6,5},{7,6},{8,15},{9,8},{10,9... | collective-permute-start | bytes 589832 | tf_op jit(solution)/shard_map/ppermute | solution.py:22
  275.2 14.9 %all-to-all-start.9 = ((f32[32,8,128]{2,1,0:T(8,128)}), f32[32,8,128]{2,1,0:T(8,128)S(1)}, u32[]{:S(2)}, u32[]{:S(2)}) async-start(f32[32,8,128]{2,1,0:T(8,128)} %tile.2), calls=%async_computation.9 | async-start | bytes 262144 | tf_op jit(solution)/shard_map/all_to_all | solution.py:26
  281.1 20.8 %collective-permute-start.20 = (f32[384,128]{1,0:T(8,128)S(1)}, f32[384,128]{1,0:T(8,128)S(1)}, u32[]{:S(2)}, u32[]{:S(2)}) collective-permute-start(f32[384,128]{1,0:T(8,128)S(1)} %get-tuple-element.96), channel_id=1, source_target_pairs={{0,8},{8,16},{16,24},{24,32},{32,40},{40,48},{48,56},{56,64},{64,7... | collective-permute-start | bytes 589832 | tf_op jit(solution)/shard_map/ppermute | solution.py:22
  282.4 19.5 %collective-permute-start.21 = (f32[384,128]{1,0:T(8,128)S(1)}, f32[384,128]{1,0:T(8,128)S(1)}, u32[]{:S(2)}, u32[]{:S(2)}) collective-permute-start(f32[384,128]{1,0:T(8,128)S(1)} %get-tuple-element.97), channel_id=1, source_target_pairs={{0,248},{8,0},{16,8},{24,16},{32,24},{40,32},{48,40},{56,48},{64,5... | collective-permute-start | bytes 589832 | tf_op jit(solution)/shard_map/ppermute | solution.py:22
  (91 other events, 517.3 us)
